TPU v7x, 32 devices: a whole 2x2x4 slice. The times are simulated.
32 devices in a mesh: gx: 4 (over x, core), gy: 8 (over z, y).
Axes of the slice: x: 2, y: 2, z: 4, core: 2. Of those that a mesh axis runs over, the one named last changes fastest.
Arguments:
- nest_state: float32 [4, 8, 96, 3072], P(None, None, 'gx', 'gy'), may hold values from -6 to 6
- parent_state: float32 [4, 8, 96, 3072], P(None, None, 'gx', 'gy'), may hold values from -6 to 6
- offset_x: int32 [1], replicated, may hold values from 1 to 15
- offset_y: int32 [1], replicated, may hold values from 385 to 511
Outputs:
- nest_out: float32 [4, 8, 96, 3072], P(None, None, 'gx', 'gy')
- parent_out: float32 [4, 8, 96, 3072], P(None, None, 'gx', 'gy')
All inputs are finite; a program needn't handle non-finite values.
Results may differ from a plain program's by a relative error of at most 0.00019.
Values sent between devices are 32-bit elements; how exact they have to be, the bound alone decides.
A program may use at most 128 MiB of HBM per device.

v0:
```python
import jax
import jax.numpy as jnp
from jax import lax
from jax.sharding import PartitionSpec as P

SUBSTEPS = 3
CARRY_RATE = 0.35
SOUND_RATE = 0.4
MIXING_RATE = 0.2


def extended(value, sides, width):
    for axis, dim in sides:
        size, length = (lax.axis_size(axis), value.shape[dim])
        up = [(i, (i + 1) % size) for i in range(size - 1)]
        down = [(j, i) for i, j in up]
        last = lax.slice_in_dim(value, length - width, length, axis=dim)
        initial = lax.slice_in_dim(value, 0, width, axis=dim)
        before = lax.ppermute(last, axis, up)
        after = lax.ppermute(initial, axis, down)
        value = jnp.concatenate([before, value, after], axis=dim)
    return value


def advance(padded):
    center = padded[:, :, 1:-1, 1:-1]
    slope_x = (padded[:, :, 2:, 1:-1] - padded[:, :, :-2, 1:-1]) * 0.5
    slope_y = (padded[:, :, 1:-1, 2:] - padded[:, :, 1:-1, :-2]) * 0.5
    carried = center[0][None] * slope_x[:3] + center[1][None] * slope_y[:3]
    potential = center[2]
    level_above = jnp.concatenate([potential[1:], potential[-1:]], axis=0)
    level_below = jnp.concatenate([potential[:1], potential[:-1]], axis=0)
    wind_east = center[0] - CARRY_RATE * carried[0] - SOUND_RATE * slope_x[3]
    wind_north = center[1] - CARRY_RATE * carried[1] - SOUND_RATE * slope_y[3]
    heat_next = (
        potential
        - CARRY_RATE * carried[2]
        + MIXING_RATE * (level_above - 2.0 * potential + level_below)
    )
    pressure = center[3] - SOUND_RATE * (slope_x[0] + slope_y[1])
    return jnp.stack([wind_east, wind_north, heat_next, pressure])


def place_along(piece, first, width, axis):
    length = piece.shape[axis]
    target = lax.broadcasted_iota(jnp.int32, (length, width), 0) - first
    places = lax.broadcasted_iota(jnp.int32, (length, width), 1)
    table = (target == places).astype(jnp.float32)
    moved = jnp.moveaxis(piece, axis, -1)
    placed = jnp.dot(
        moved, table, precision=lax.Precision.HIGHEST, preferred_element_type=jnp.float32
    )
    return jnp.moveaxis(placed, -1, axis)


def on_device(nest_state, parent_state, offset_x, offset_y):
    shift_x = offset_x[0]
    shift_y = offset_y[0]
    count_x = lax.axis_size("gx")
    count_y = lax.axis_size("gy")
    index_x = lax.axis_index("gx")
    index_y = lax.axis_index("gy")
    levels = nest_state.shape[1]
    nest_cols = nest_state.shape[2]
    nest_rows = nest_state.shape[3]
    parent_cols = parent_state.shape[2]
    parent_rows = parent_state.shape[3]
    coarse_cols = nest_cols // 3
    coarse_rows = nest_rows // 3
    span_x = count_x * coarse_cols
    span_y = count_y * coarse_rows

    def take_slab(wanted, owner_index, extent, axis):
        local = wanted - owner_index * extent
        inside = (local >= 0) & (local < extent)
        slab = lax.dynamic_slice_in_dim(parent_state, jnp.clip(local, 0, extent - 1), 1, axis)
        return jnp.where(inside, jnp.squeeze(slab, axis), 0.0)

    columns = jnp.stack(
        [
            take_slab(shift_x - 1, index_x, parent_cols, 2),
            take_slab(shift_x + span_x, index_x, parent_cols, 2),
        ]
    )
    columns = lax.psum(columns, "gx")
    row_pair = jnp.stack(
        [
            take_slab(shift_y - 1, index_y, parent_rows, 3),
            take_slab(shift_y + span_y, index_y, parent_rows, 3),
        ]
    )
    row_pair = lax.psum(row_pair, "gy")
    column_first = shift_y + index_y * coarse_rows - 1
    row_first = shift_x + index_x * coarse_cols - 1
    column_strip = place_along(
        lax.all_gather(columns, "gy", axis=3, tiled=True), column_first, coarse_rows + 2, 3
    )
    row_strip = place_along(
        lax.all_gather(row_pair, "gx", axis=3, tiled=True), row_first, coarse_cols + 2, 3
    )
    column_strip = jnp.repeat(column_strip, 3, axis=3)
    row_strip = jnp.repeat(row_strip, 3, axis=3)
    parent_padded = extended(parent_state, (("gx", 2), ("gy", 3)), 1)
    parent_next = advance(parent_padded)
    fields = nest_state
    for substep in range(SUBSTEPS):
        padded = extended(fields, (("gx", 2), ("gy", 3)), 1)
        col_pos = lax.broadcasted_iota(jnp.int32, (padded.shape[2], 1), 0)
        row_pos = lax.broadcasted_iota(jnp.int32, (1, padded.shape[3]), 1)
        lower = 3 - 1
        west = column_strip[0][:, :, None, lower : lower + nest_rows + 2 * 1]
        east = column_strip[1][:, :, None, lower : lower + nest_rows + 2 * 1]
        south = row_strip[0][:, :, lower : lower + nest_cols + 2 * 1, None]
        north = row_strip[1][:, :, lower : lower + nest_cols + 2 * 1, None]
        result = jnp.where((index_x == 0) & (col_pos < 1), west, padded)
        result = jnp.where((index_x == count_x - 1) & (col_pos >= nest_cols + 1), east, result)
        result = jnp.where((index_y == 0) & (row_pos < 1), south, result)
        result = jnp.where((index_y == count_y - 1) & (row_pos >= nest_rows + 1), north, result)
        fields = advance(result)
    coarse = fields[:3].reshape(3, levels, coarse_cols, 3, coarse_rows, 3).mean(axis=(3, 5))
    col_first = index_x * parent_cols - shift_x
    rows_first = index_y * parent_rows - shift_y
    partial_block = place_along(
        lax.all_gather(coarse, "gy", axis=3, tiled=True), rows_first, parent_rows, 3
    )
    returned = place_along(
        lax.all_gather(partial_block, "gx", axis=2, tiled=True), col_first, parent_cols, 2
    )
    col_global = index_x * parent_cols + lax.broadcasted_iota(jnp.int32, (parent_cols, 1), 0)
    row_global = index_y * parent_rows + lax.broadcasted_iota(jnp.int32, (1, parent_rows), 1)
    inside = (
        (col_global >= shift_x)
        & (col_global < shift_x + span_x)
        & (row_global >= shift_y)
        & (row_global < shift_y + span_y)
    )
    blended = jnp.where(inside, returned, parent_next[:3])
    parent_out = jnp.concatenate([blended, parent_next[3:]], axis=0)
    return (fields, parent_out)


def solution(mesh):
    placed = (P(None, None, "gx", "gy"), P(None, None, "gx", "gy"), P(), P())
    return jax.shard_map(
        on_device,
        mesh=mesh,
        in_specs=placed,
        out_specs=(P(None, None, "gx", "gy"), P(None, None, "gx", "gy")),
        check_vma=False,
    )
```

profile of v0, /device:TPU:0, one launch (start us, length us, event | category | flops | bytes accessed | tf_op | source)
XLA Modules:
  0.0 323.4 jit_solution(11506212641012016978)
XLA Ops:
  8.0 2.2 fusion.95
  12.1 2.4 collective-permute-start
  17.4 39.1 %psum.14 = f32[2,4,8,24]{2,1,0,3:T(4,128)S(1)} all-reduce(f32[2,4,8,24]{2,1,0,3:T(4,128)S(1)} %copy.41), channel_id=1, replica_groups=mesh['gx'=4,'gy'=8] {'gy'}, use_global_device_ids=true, to_apply=%region_0.1 | all-reduce | flops 1536 | bytes 12288 | tf_op jit(solution)/shard_map/psum | solution.py:92
  56.5 9.2 %all_gather.12 = f32[2,4,8,96]{2,1,0,3:T(4,128)S(1)} all-gather(f32[2,4,8,24]{2,1,0,3:T(4,128)S(1)} %psum.14), channel_id=1, replica_groups=mesh['gx'=4,'gy'=8] {'gx'}, dimensions={3}, use_global_device_ids=true | all-gather | bytes 30720 | tf_op jit(solution)/shard_map/all_gather | solution.py:99
  67.9 2.1 collective-permute-start.2
  71.3 50.3 %all_gather.13 = f32[2,4,8,3072]{3,2,1,0:T(8,128)S(1)} all-gather(f32[2,4,8,384]{3,2,1,0:T(8,128)} %all-reduce.2.cloned.1.call-done), channel_id=1, replica_groups=mesh['gx'=4,'gy'=8] {'gy'}, dimensions={3}, use_global_device_ids=true | all-gather | bytes 884736 | tf_op jit(solution)/shard_map/all_gather | solution.py:96
  124.2 3.1 fusion.2
  133.5 5.1 %collective-permute-start.13 = (f32[4,8,1,384]{3,2,1,0:T(1,128)}, f32[4,8,1,384]{3,2,1,0:T(1,128)S(1)}, u32[]{:S(2)}, u32[]{:S(2)}) collective-permute-start(f32[4,8,1,384]{3,2,1,0:T(1,128)} %get-tuple-element.58), channel_id=1, source_target_pairs={{0,8},{8,16},{16,24},{1,9},{9,17},{17,25},{2,10},{10,18},{18,26},{... | collective-permute-start | bytes 147464 | tf_op jit(solution)/shard_map/ppermute | solution.py:19
  142.6 20.1 %collective-permute-done.6 = f32[4,8,26,1]{3,2,1,0:T(8,128)S(1)} collective-permute-done((f32[4,8,26,1]{3,2,1,0:T(8,128)S(1)}, f32[4,8,26,1]{3,2,1,0:T(8,128)S(1)}, u32[]{:S(2)}, u32[]{:S(2)}) %collective-permute-start.6) | collective-permute-done | bytes 3360 | tf_op jit(solution)/shard_map/ppermute | solution.py:19
  162.7 2.6 fusion.5
  167.7 3.1 collective-permute-start.8
  172.7 1.5 collective-permute-done.9
  174.5 4.4 %collective-permute-start.10 = (f32[4,8,26,1]{3,2,1,0:T(8,128)S(1)}, f32[4,8,26,1]{3,2,1,0:T(8,128)S(1)}, u32[]{:S(2)}, u32[]{:S(2)}) collective-permute-start(f32[4,8,26,1]{3,2,1,0:T(8,128)S(1)} %get-tuple-element.46), channel_id=1, source_target_pairs={{0,1},{1,2},{2,3},{3,4},{4,5},{5,6},{6,7},{8,9},{9,10},{10,11},{11... | collective-permute-start | bytes 9992 | tf_op jit(solution)/shard_map/ppermute | solution.py:19
  180.3 20.3 %collective-permute-done.10 = f32[4,8,26,1]{3,2,1,0:T(8,128)S(1)} collective-permute-done((f32[4,8,26,1]{3,2,1,0:T(8,128)S(1)}, f32[4,8,26,1]{3,2,1,0:T(8,128)S(1)}, u32[]{:S(2)}, u32[]{:S(2)}) %collective-permute-start.10) | collective-permute-done | bytes 3360 | tf_op jit(solution)/shard_map/ppermute | solution.py:19
  200.6 2.6 fusion.8
  206.2 8.3 %copy.53 = f32[3,8,24,384]{1,3,2,0:T(8,128)} copy(f32[3,8,24,384]{3,2,1,0:T(8,128)S(1)} %pad_maximum_fusion.10) | data formatting | bytes 1769472 | tf_op jit(solution)/shard_map/stack | solution.py:41
  214.4 21.9 %reshape.170 = f32[3,8,8,3,128,3]{1,5,4,3,2,0:T(4,128)} reshape(f32[3,8,24,384]{1,3,2,0:T(8,128)} %copy.53) | data formatting | bytes 1769472 | tf_op jit(solution)/shard_map/reshape | solution.py:120
  236.3 14.8 %reduce_sum.9 = f32[3,8,8,128]{1,3,2,0:T(8,128)S(1)} reduce(f32[3,8,8,3,128,3]{1,5,4,3,2,0:T(4,128)} %reshape.170, f32[]{:T(128)} %constant.17.clone.1), dimensions={3,5}, to_apply=%region_2.3 | reduce | flops 196608 | bytes 983044 | tf_op jit(solution)/shard_map/reduce_sum | solution.py:120
  251.6 36.0 %all_gather.14 = f32[3,8,8,1024]{3,2,1,0:T(8,128)S(1)} all-gather(f32[3,8,8,128]{3,2,1,0:T(8,128)S(1)} %broadcast_multiply_fusion), channel_id=1, replica_groups=mesh['gx'=4,'gy'=8] {'gy'}, dimensions={3}, use_global_device_ids=true | all-gather | bytes 884736 | tf_op jit(solution)/shard_map/all_gather | solution.py:124
  287.6 1.7 fusion.13
  291.1 4.6 %collective-permute-start.15 = (f32[4,8,26,1]{3,2,1,0:T(8,128)S(1)}, f32[4,8,26,1]{3,2,1,0:T(8,128)S(1)}, u32[]{:S(2)}, u32[]{:S(2)}) collective-permute-start(f32[4,8,26,1]{3,2,1,0:T(8,128)S(1)} %get-tuple-element.45), channel_id=1, source_target_pairs={{0,1},{1,2},{2,3},{3,4},{4,5},{5,6},{6,7},{8,9},{9,10},{10,11},{11... | collective-permute-start | bytes 9992 | tf_op jit(solution)/shard_map/ppermute | solution.py:19
  295.7 5.2 %collective-permute-done.14 = f32[4,8,26,1]{3,2,1,0:T(8,128)S(1)} collective-permute-done((f32[4,8,26,1]{3,2,1,0:T(8,128)S(1)}, f32[4,8,26,1]{3,2,1,0:T(8,128)S(1)}, u32[]{:S(2)}, u32[]{:S(2)}) %collective-permute-start.14) | collective-permute-done | bytes 3360 | tf_op jit(solution)/shard_map/ppermute | solution.py:20
  300.9 8.2 %collective-permute-done.15 = f32[4,8,26,1]{3,2,1,0:T(8,128)S(1)} collective-permute-done((f32[4,8,26,1]{3,2,1,0:T(8,128)S(1)}, f32[4,8,26,1]{3,2,1,0:T(8,128)S(1)}, u32[]{:S(2)}, u32[]{:S(2)}) %collective-permute-start.15) | collective-permute-done | bytes 3360 | tf_op jit(solution)/shard_map/ppermute | solution.py:19
  313.6 1.8 fusion.15
  (120 shorter events, 36.8 us)
Async XLA Ops:
  7.2 9.3 %copy-start = (f32[4,8,24,384]{3,2,1,0:T(8,128)S(1)}, f32[4,8,24,384]{3,2,1,0:T(8,128)}, u32[]{:S(2)}) copy-start(f32[4,8,24,384]{3,2,1,0:T(8,128)} %param.5) | copy-start | bytes 3538948
  7.2 64.1 %all-reduce.2.cloned.1.call-start = ((), (), s32[]{:S(2)}) async-start(), calls=%async_computation | async-start | bytes 196608 | tf_op jit(solution)/shard_map/psum | solution.py:85
  10.8 302.8 %all-gather.2.cloned.1.call-start = ((), (), s32[]{:S(2)}) async-start(), calls=%async_computation.1 | async-start | bytes 1474560 | tf_op jit(solution)/shard_map/all_gather | solution.py:127
  12.1 54.6 %collective-permute-start = (f32[4,8,1,384]{3,2,1,0:T(1,128)S(1)}, f32[4,8,1,384]{3,2,1,0:T(1,128)S(1)}, u32[]{:S(2)}, u32[]{:S(2)}) collective-permute-start(f32[4,8,1,384]{3,2,1,0:T(1,128)S(1)} %get-tuple-element.68), channel_id=1, source_target_pairs={{0,8},{8,16},{16,24},{1,9},{9,17},{17,25},{2,10},{10,18},{18,26},{... | collective-permute-start | bytes 147464 | tf_op jit(solution)/shard_map/ppermute | solution.py:19
  14.4 52.2 %collective-permute-start.1 = (f32[4,8,1,384]{3,2,1,0:T(1,128)S(1)}, f32[4,8,1,384]{3,2,1,0:T(1,128)S(1)}, u32[]{:S(2)}, u32[]{:S(2)}) collective-permute-start(f32[4,8,1,384]{3,2,1,0:T(1,128)S(1)} %get-tuple-element.69), channel_id=1, source_target_pairs={{8,0},{16,8},{24,16},{9,1},{17,9},{25,17},{10,2},{18,10},{26,18},{... | collective-permute-start | bytes 147464 | tf_op jit(solution)/shard_map/ppermute | solution.py:20
  17.0 49.7 %copy-start.1 = (f32[4,8,24,384]{3,2,1,0:T(8,128)S(1)}, f32[4,8,24,384]{3,2,1,0:T(8,128)}, u32[]{:S(2)}) copy-start(f32[4,8,24,384]{3,2,1,0:T(8,128)} %param.4) | copy-start | bytes 3538948
  67.9 56.3 %collective-permute-start.2 = (f32[4,8,26,1]{3,2,1,0:T(8,128)}, f32[4,8,26,1]{3,2,1,0:T(8,128)}, u32[]{:S(2)}, u32[]{:S(2)}) collective-permute-start(f32[4,8,26,1]{3,2,1,0:T(8,128)} %get-tuple-element.50), channel_id=1, source_target_pairs={{0,1},{1,2},{2,3},{3,4},{4,5},{5,6},{6,7},{8,9},{9,10},{10,11},{11... | collective-permute-start | bytes 9992 | tf_op jit(solution)/shard_map/ppermute | solution.py:19
  70.0 54.2 %collective-permute-start.3 = (f32[4,8,26,1]{3,2,1,0:T(8,128)}, f32[4,8,26,1]{3,2,1,0:T(8,128)}, u32[]{:S(2)}, u32[]{:S(2)}) collective-permute-start(f32[4,8,26,1]{3,2,1,0:T(8,128)} %get-tuple-element.51), channel_id=1, source_target_pairs={{1,0},{2,1},{3,2},{4,3},{5,4},{6,5},{7,6},{9,8},{10,9},{11,10},{12... | collective-permute-start | bytes 9992 | tf_op jit(solution)/shard_map/ppermute | solution.py:20
  129.6 9.0 %collective-permute-start.4 = (f32[4,8,1,384]{3,2,1,0:T(1,128)S(1)}, f32[4,8,1,384]{3,2,1,0:T(1,128)S(1)}, u32[]{:S(2)}, u32[]{:S(2)}) collective-permute-start(f32[4,8,1,384]{3,2,1,0:T(1,128)S(1)} %get-tuple-element.64), channel_id=1, source_target_pairs={{0,8},{8,16},{16,24},{1,9},{9,17},{17,25},{2,10},{10,18},{18,26},{... | collective-permute-start | bytes 147464 | tf_op jit(solution)/shard_map/ppermute | solution.py:19
  130.9 7.7 %collective-permute-start.5 = (f32[4,8,1,384]{3,2,1,0:T(1,128)S(1)}, f32[4,8,1,384]{3,2,1,0:T(1,128)S(1)}, u32[]{:S(2)}, u32[]{:S(2)}) collective-permute-start(f32[4,8,1,384]{3,2,1,0:T(1,128)S(1)} %get-tuple-element.65), channel_id=1, source_target_pairs={{8,0},{16,8},{24,16},{9,1},{17,9},{25,17},{10,2},{18,10},{26,18},{... | collective-permute-start | bytes 147464 | tf_op jit(solution)/shard_map/ppermute | solution.py:20
  132.2 157.3 %collective-permute-start.12 = (f32[4,8,1,384]{3,2,1,0:T(1,128)}, f32[4,8,1,384]{3,2,1,0:T(1,128)S(1)}, u32[]{:S(2)}, u32[]{:S(2)}) collective-permute-start(f32[4,8,1,384]{3,2,1,0:T(1,128)} %get-tuple-element.59), channel_id=1, source_target_pairs={{8,0},{16,8},{24,16},{9,1},{17,9},{25,17},{10,2},{18,10},{26,18},{... | collective-permute-start | bytes 147464 | tf_op jit(solution)/shard_map/ppermute | solution.py:20
  133.5 156.0 %collective-permute-start.13 = (f32[4,8,1,384]{3,2,1,0:T(1,128)}, f32[4,8,1,384]{3,2,1,0:T(1,128)S(1)}, u32[]{:S(2)}, u32[]{:S(2)}) collective-permute-start(f32[4,8,1,384]{3,2,1,0:T(1,128)} %get-tuple-element.58), channel_id=1, source_target_pairs={{0,8},{8,16},{16,24},{1,9},{9,17},{17,25},{2,10},{10,18},{18,26},{... | collective-permute-start | bytes 147464 | tf_op jit(solution)/shard_map/ppermute | solution.py:19
  138.9 23.8 %collective-permute-start.6 = (f32[4,8,26,1]{3,2,1,0:T(8,128)S(1)}, f32[4,8,26,1]{3,2,1,0:T(8,128)S(1)}, u32[]{:S(2)}, u32[]{:S(2)}) collective-permute-start(f32[4,8,26,1]{3,2,1,0:T(8,128)S(1)} %get-tuple-element.48), channel_id=1, source_target_pairs={{0,1},{1,2},{2,3},{3,4},{4,5},{5,6},{6,7},{8,9},{9,10},{10,11},{11... | collective-permute-start | bytes 9992 | tf_op jit(solution)/shard_map/ppermute | solution.py:19
  140.3 22.5 %collective-permute-start.7 = (f32[4,8,26,1]{3,2,1,0:T(8,128)S(1)}, f32[4,8,26,1]{3,2,1,0:T(8,128)S(1)}, u32[]{:S(2)}, u32[]{:S(2)}) collective-permute-start(f32[4,8,26,1]{3,2,1,0:T(8,128)S(1)} %get-tuple-element.49), channel_id=1, source_target_pairs={{1,0},{2,1},{3,2},{4,3},{5,4},{6,5},{7,6},{9,8},{10,9},{11,10},{12... | collective-permute-start | bytes 9992 | tf_op jit(solution)/shard_map/ppermute | solution.py:20
  167.7 5.0 %collective-permute-start.8 = (f32[4,8,1,384]{3,2,1,0:T(1,128)S(1)}, f32[4,8,1,384]{3,2,1,0:T(1,128)S(1)}, u32[]{:S(2)}, u32[]{:S(2)}) collective-permute-start(f32[4,8,1,384]{3,2,1,0:T(1,128)S(1)} %get-tuple-element.62), channel_id=1, source_target_pairs={{0,8},{8,16},{16,24},{1,9},{9,17},{17,25},{2,10},{10,18},{18,26},{... | collective-permute-start | bytes 147464 | tf_op jit(solution)/shard_map/ppermute | solution.py:19
  170.8 3.4 %collective-permute-start.9 = (f32[4,8,1,384]{3,2,1,0:T(1,128)S(1)}, f32[4,8,1,384]{3,2,1,0:T(1,128)S(1)}, u32[]{:S(2)}, u32[]{:S(2)}) collective-permute-start(f32[4,8,1,384]{3,2,1,0:T(1,128)S(1)} %get-tuple-element.63), channel_id=1, source_target_pairs={{8,0},{16,8},{24,16},{9,1},{17,9},{25,17},{10,2},{18,10},{26,18},{... | collective-permute-start | bytes 147464 | tf_op jit(solution)/shard_map/ppermute | solution.py:20
  174.5 26.0 %collective-permute-start.10 = (f32[4,8,26,1]{3,2,1,0:T(8,128)S(1)}, f32[4,8,26,1]{3,2,1,0:T(8,128)S(1)}, u32[]{:S(2)}, u32[]{:S(2)}) collective-permute-start(f32[4,8,26,1]{3,2,1,0:T(8,128)S(1)} %get-tuple-element.46), channel_id=1, source_target_pairs={{0,1},{1,2},{2,3},{3,4},{4,5},{5,6},{6,7},{8,9},{9,10},{10,11},{11... | collective-permute-start | bytes 9992 | tf_op jit(solution)/shard_map/ppermute | solution.py:19
  178.9 21.6 %collective-permute-start.11 = (f32[4,8,26,1]{3,2,1,0:T(8,128)S(1)}, f32[4,8,26,1]{3,2,1,0:T(8,128)S(1)}, u32[]{:S(2)}, u32[]{:S(2)}) collective-permute-start(f32[4,8,26,1]{3,2,1,0:T(8,128)S(1)} %get-tuple-element.47), channel_id=1, source_target_pairs={{1,0},{2,1},{3,2},{4,3},{5,4},{6,5},{7,6},{9,8},{10,9},{11,10},{12... | collective-permute-start | bytes 9992 | tf_op jit(solution)/shard_map/ppermute | solution.py:20
  206.1 8.3 %copy-start.2 = (f32[1,8,24,384]{3,2,1,0:T(8,128)}, f32[1,8,24,384]{3,2,1,0:T(8,128)S(1)}, u32[]{:S(2)}) copy-start(f32[1,8,24,384]{3,2,1,0:T(8,128)S(1)} %get-tuple-element.11) | copy-start | bytes 884740
  289.8 11.1 %collective-permute-start.14 = (f32[4,8,26,1]{3,2,1,0:T(8,128)S(1)}, f32[4,8,26,1]{3,2,1,0:T(8,128)S(1)}, u32[]{:S(2)}, u32[]{:S(2)}) collective-permute-start(f32[4,8,26,1]{3,2,1,0:T(8,128)S(1)} %get-tuple-element.44), channel_id=1, source_target_pairs={{1,0},{2,1},{3,2},{4,3},{5,4},{6,5},{7,6},{9,8},{10,9},{11,10},{12... | collective-permute-start | bytes 9992 | tf_op jit(solution)/shard_map/ppermute | solution.py:20
  291.1 18.0 %collective-permute-start.15 = (f32[4,8,26,1]{3,2,1,0:T(8,128)S(1)}, f32[4,8,26,1]{3,2,1,0:T(8,128)S(1)}, u32[]{:S(2)}, u32[]{:S(2)}) collective-permute-start(f32[4,8,26,1]{3,2,1,0:T(8,128)S(1)} %get-tuple-element.45), channel_id=1, source_target_pairs={{0,1},{1,2},{2,3},{3,4},{4,5},{5,6},{6,7},{8,9},{9,10},{10,11},{11... | collective-permute-start | bytes 9992 | tf_op jit(solution)/shard_map/ppermute | solution.py:19
  310.4 1.1 copy-start.7
  310.4 1.1 copy-start.8
  312.5 1.1 copy-start.5
  (4 other events, 4.1 us)
Sparse Core Ops, SparseCore 0:
  11.0 34.0 all-reduce.1
  289.5 15.4 all-gather.1
where the time goes:
time: 325 us; the launch traced here: 323 us
  blocking collectives  135 us (42%)
  waiting for transfers between devices  55.4 us (17%)
  local copies, waits for them, and re-layouts  40.7 us (13%)
  other arithmetic  36.6 us (11%)
  starting transfers between devices  34.8 us (11%)
  between operations  16.1 us (5%)
  matrix products  5.11 us (2%)
    all_gather x1, blocking collectives, on_device(): lax.all_gather(columns, 'gy', axis=3, tiled=True)  50.3 us
    ppermute x8, waiting for transfers between devices, extended(): before = lax.ppermute(last, axis, up)  48.7 us
    psum x1, blocking collectives, on_device(): row_pair = lax.psum(row_pair, 'gy')  39.1 us
    all_gather x1, blocking collectives, on_device(): lax.all_gather(coarse, 'gy', axis=3, tiled=True)  36 us
    ppermute x8, starting transfers between devices, extended(): before = lax.ppermute(last, axis, up)  24.2 us
    reshape x1, local copies, waits for them, and re-layouts, on_device(): fields[:3].reshape(3, levels, coarse_cols, 3, coarse_rows, 3)  21.9 us
    reduce_sum x1, other arithmetic, on_device(): fields[:3].reshape(3, levels, coarse_cols, 3, coarse_rows, 3)  14.8 us
    ppermute x8, starting transfers between devices, extended(): after = lax.ppermute(initial, axis, down)  10.5 us
  transfers between devices with their start and end apart: 18, of which 5 were waited for; matrix products, arithmetic and copies ran while one was open for 22% of the time, Pallas kernels for 0%

commit v1 on v0

--- a/solution.py
+++ b/solution.py
@@ -89,7 +89,9 @@
             take_slab(shift_y + span_y, index_y, parent_rows, 3),
         ]
     )
-    row_pair = lax.psum(row_pair, "gy")
+    row_pair = row_pair
+    for hop in (1, 2, 4):
+        row_pair = row_pair + lax.ppermute(row_pair, "gy", [(dev, dev ^ hop) for dev in range(8)])
     column_first = shift_y + index_y * coarse_rows - 1
     row_first = shift_x + index_x * coarse_cols - 1
     column_strip = place_along(

time: 325 us -> 300 us (0.923)
  blocking collectives: 135 us -> 93.4 us
  starting transfers between devices: 34.8 us -> 44.6 us
  waiting for transfers between devices: 55.4 us -> 63 us
    psum x1 -> x0, blocking collectives: 39.1 us -> none  [on_device(): row_pair = lax.psum(row_pair, 'gy')]
    ppermute x8, waiting for transfers between devices: 48.7 us -> 36.2 us  [extended(): before = lax.ppermute(last, axis, up)]
    ppermute x8, waiting for transfers between devices: 6.69 us -> 15.7 us  [extended(): after = lax.ppermute(initial, axis, down)]
    ppermute x0 -> x3, waiting for transfers between devices: none -> 8.63 us  [on_device(): lax.ppermute(row_pair, 'gy', [(dev, dev ^ hop) for dev in range(8)])]
    ppermute x0 -> x3, starting transfers between devices: none -> 7.33 us  [on_device(): lax.ppermute(row_pair, 'gy', [(dev, dev ^ hop) for dev in range(8)])]
  transfers between devices with their start and end apart: 18 -> 21, of which waited for: 5 -> 9; matrix products, arithmetic and copies ran while one was open for 22% -> 23% of each run, Pallas kernels for 0% -> 0%
where the time goes in v1:
time: 300 us; the launch traced here: 298 us
  blocking collectives  93.4 us (31%)
  waiting for transfers between devices  63 us (21%)
  starting transfers between devices  44.6 us (15%)
  local copies, waits for them, and re-layouts  39.5 us (13%)
  other arithmetic  36.5 us (12%)
  between operations  16 us (5%)
  matrix products  5.1 us (2%)
    all_gather x1, blocking collectives, on_device(): lax.all_gather(columns, 'gy', axis=3, tiled=True)  50.5 us
    all_gather x1, blocking collectives, on_device(): lax.all_gather(coarse, 'gy', axis=3, tiled=True)  36.3 us
    ppermute x8, waiting for transfers between devices, extended(): before = lax.ppermute(last, axis, up)  36.2 us
    ppermute x8, starting transfers between devices, extended(): before = lax.ppermute(last, axis, up)  26.9 us
    reshape x1, local copies, waits for them, and re-layouts, on_device(): fields[:3].reshape(3, levels, coarse_cols, 3, coarse_rows, 3)  21.9 us
    ppermute x8, waiting for transfers between devices, extended(): after = lax.ppermute(initial, axis, down)  15.7 us
    reduce_sum x1, other arithmetic, on_device(): fields[:3].reshape(3, levels, coarse_cols, 3, coarse_rows, 3)  14.8 us
    ppermute x8, starting transfers between devices, extended(): after = lax.ppermute(initial, axis, down)  10.3 us
  transfers between devices with their start and end apart: 21, of which 9 were waited for; matrix products, arithmetic and copies ran while one was open for 23% of the time, Pallas kernels for 0%

profile of v1, /device:TPU:0, one launch (start us, length us, event | category | flops | bytes accessed | tf_op | source)
XLA Modules:
  0.0 298.1 jit_solution(8221006339014456606)
XLA Ops:
  10.0 3.0 %collective-permute-start = (f32[2,4,8,24]{2,1,0,3:T(4,128)S(1)}, f32[2,4,8,24]{2,1,0,3:T(4,128)S(1)}, u32[]{:S(2)}, u32[]{:S(2)}) collective-permute-start(f32[2,4,8,24]{2,1,0,3:T(4,128)S(1)} %copy.42), channel_id=1, source_target_pairs={{0,1},{1,0},{2,3},{3,2},{4,5},{5,4},{6,7},{7,6},{8,9},{9,8},{10,11... | collective-permute-start | bytes 18440 | tf_op jit(solution)/shard_map/ppermute | solution.py:94
  19.9 3.0 %collective-permute-done.1 = f32[2,4,8,24]{2,1,0,3:T(4,128)S(1)} collective-permute-done((f32[2,4,8,24]{2,1,0,3:T(4,128)S(1)}, f32[2,4,8,24]{2,1,0,3:T(4,128)S(1)}, u32[]{:S(2)}, u32[]{:S(2)}) %collective-permute-start.1) | collective-permute-done | bytes 6176 | tf_op jit(solution)/shard_map/ppermute | solution.py:94
  22.9 2.7 collective-permute-start.2
  25.6 5.6 %collective-permute-done.2 = f32[2,4,8,24]{2,1,0,3:T(4,128)S(1)} collective-permute-done((f32[2,4,8,24]{2,1,0,3:T(4,128)S(1)}, f32[2,4,8,24]{2,1,0,3:T(4,128)S(1)}, u32[]{:S(2)}, u32[]{:S(2)}) %collective-permute-start.2) | collective-permute-done | bytes 6176 | tf_op jit(solution)/shard_map/ppermute | solution.py:94
  31.2 6.6 %all_gather.12 = f32[2,4,8,96]{2,1,0,3:T(4,128)S(1)} all-gather(f32[2,4,8,24]{2,1,0,3:T(4,128)S(1)} %add.121), channel_id=1, replica_groups=mesh['gx'=4,'gy'=8] {'gx'}, dimensions={3}, use_global_device_ids=true | all-gather | bytes 30720 | tf_op jit(solution)/shard_map/all_gather | solution.py:101
  40.0 3.2 %collective-permute-start.5 = (f32[4,8,26,1]{3,2,1,0:T(8,128)}, f32[4,8,26,1]{3,2,1,0:T(8,128)}, u32[]{:S(2)}, u32[]{:S(2)}) collective-permute-start(f32[4,8,26,1]{3,2,1,0:T(8,128)} %get-tuple-element.50), channel_id=1, source_target_pairs={{0,1},{1,2},{2,3},{3,4},{4,5},{5,6},{6,7},{8,9},{9,10},{10,11},{11... | collective-permute-start | bytes 9992 | tf_op jit(solution)/shard_map/ppermute | solution.py:19
  44.5 2.5 all-reduce.2.cloned.1.call-done
  47.0 50.5 %all_gather.13 = f32[2,4,8,3072]{3,2,1,0:T(8,128)S(1)} all-gather(f32[2,4,8,384]{3,2,1,0:T(8,128)} %all-reduce.2.cloned.1.call-done), channel_id=1, replica_groups=mesh['gx'=4,'gy'=8] {'gy'}, dimensions={3}, use_global_device_ids=true | all-gather | bytes 884736 | tf_op jit(solution)/shard_map/all_gather | solution.py:98
  100.0 3.1 %fusion.2 = f32[4,8,26,386]{3,2,1,0:T(8,128)S(1)} fusion(f32[4,8,26,1]{3,2,1,0:T(8,128)} %collective-permute-done.6, f32[4,8,1,384]{3,2,1,0:T(1,128)S(1)} %collective-permute-done.4, f32[4,8,24,384]{3,2,1,0:T(8,128)S(1)} %copy-done.1, f32[4,8,1,384]{3,2,1,0:T(1,128)S(1)} %collective-permute-done.3, f32[4,8,26,1]{3,2,1,0:T(8,128)} %collective-permute-done.5, ...), kind=kLoop, calls=%fused_computation.3 | loop fusion | flops 2569216 | bytes 2675512 | tf_op jit(solution)/shard_map/jit(_where)/select_n | solution.py:120
  109.3 5.1 %collective-permute-start.16 = (f32[4,8,1,384]{3,2,1,0:T(1,128)}, f32[4,8,1,384]{3,2,1,0:T(1,128)S(1)}, u32[]{:S(2)}, u32[]{:S(2)}) collective-permute-start(f32[4,8,1,384]{3,2,1,0:T(1,128)} %get-tuple-element.58), channel_id=1, source_target_pairs={{0,8},{8,16},{16,24},{1,9},{9,17},{17,25},{2,10},{10,18},{18,26},{... | collective-permute-start | bytes 147464 | tf_op jit(solution)/shard_map/ppermute | solution.py:19
  116.0 4.8 %collective-permute-start.9 = (f32[4,8,26,1]{3,2,1,0:T(8,128)S(1)}, f32[4,8,26,1]{3,2,1,0:T(8,128)S(1)}, u32[]{:S(2)}, u32[]{:S(2)}) collective-permute-start(f32[4,8,26,1]{3,2,1,0:T(8,128)S(1)} %get-tuple-element.48), channel_id=1, source_target_pairs={{0,1},{1,2},{2,3},{3,4},{4,5},{5,6},{6,7},{8,9},{9,10},{10,11},{11... | collective-permute-start | bytes 9992 | tf_op jit(solution)/shard_map/ppermute | solution.py:19
  121.6 9.0 %collective-permute-done.10 = f32[4,8,26,1]{3,2,1,0:T(8,128)S(1)} collective-permute-done((f32[4,8,26,1]{3,2,1,0:T(8,128)S(1)}, f32[4,8,26,1]{3,2,1,0:T(8,128)S(1)}, u32[]{:S(2)}, u32[]{:S(2)}) %collective-permute-start.10) | collective-permute-done | bytes 3360 | tf_op jit(solution)/shard_map/ppermute | solution.py:20
  130.6 7.7 %collective-permute-done.9 = f32[4,8,26,1]{3,2,1,0:T(8,128)S(1)} collective-permute-done((f32[4,8,26,1]{3,2,1,0:T(8,128)S(1)}, f32[4,8,26,1]{3,2,1,0:T(8,128)S(1)}, u32[]{:S(2)}, u32[]{:S(2)}) %collective-permute-start.9) | collective-permute-done | bytes 3360 | tf_op jit(solution)/shard_map/ppermute | solution.py:19
  138.3 2.6 fusion.5
  149.0 4.4 %collective-permute-start.13 = (f32[4,8,26,1]{3,2,1,0:T(8,128)S(1)}, f32[4,8,26,1]{3,2,1,0:T(8,128)S(1)}, u32[]{:S(2)}, u32[]{:S(2)}) collective-permute-start(f32[4,8,26,1]{3,2,1,0:T(8,128)S(1)} %get-tuple-element.46), channel_id=1, source_target_pairs={{0,1},{1,2},{2,3},{3,4},{4,5},{5,6},{6,7},{8,9},{9,10},{10,11},{11... | collective-permute-start | bytes 9992 | tf_op jit(solution)/shard_map/ppermute | solution.py:19
  154.8 20.3 %collective-permute-done.13 = f32[4,8,26,1]{3,2,1,0:T(8,128)S(1)} collective-permute-done((f32[4,8,26,1]{3,2,1,0:T(8,128)S(1)}, f32[4,8,26,1]{3,2,1,0:T(8,128)S(1)}, u32[]{:S(2)}, u32[]{:S(2)}) %collective-permute-start.13) | collective-permute-done | bytes 3360 | tf_op jit(solution)/shard_map/ppermute | solution.py:19
  175.1 2.6 fusion.8
  180.7 8.3 %copy.54 = f32[3,8,24,384]{1,3,2,0:T(8,128)} copy(f32[3,8,24,384]{3,2,1,0:T(8,128)S(1)} %pad_maximum_fusion.10) | data formatting | bytes 1769472 | tf_op jit(solution)/shard_map/stack | solution.py:41
  188.9 21.9 %reshape.170 = f32[3,8,8,3,128,3]{1,5,4,3,2,0:T(4,128)} reshape(f32[3,8,24,384]{1,3,2,0:T(8,128)} %copy.54) | data formatting | bytes 1769472 | tf_op jit(solution)/shard_map/reshape | solution.py:122
  210.8 14.8 %reduce_sum.9 = f32[3,8,8,128]{1,3,2,0:T(8,128)S(1)} reduce(f32[3,8,8,3,128,3]{1,5,4,3,2,0:T(4,128)} %reshape.170, f32[]{:T(128)} %constant.17.clone.1), dimensions={3,5}, to_apply=%region_1.2 | reduce | flops 196608 | bytes 983044 | tf_op jit(solution)/shard_map/reduce_sum | solution.py:122
  226.1 36.3 %all_gather.14 = f32[3,8,8,1024]{3,2,1,0:T(8,128)S(1)} all-gather(f32[3,8,8,128]{3,2,1,0:T(8,128)S(1)} %broadcast_multiply_fusion), channel_id=1, replica_groups=mesh['gx'=4,'gy'=8] {'gy'}, dimensions={3}, use_global_device_ids=true | all-gather | bytes 884736 | tf_op jit(solution)/shard_map/all_gather | solution.py:126
  265.9 4.6 %collective-permute-start.18 = (f32[4,8,26,1]{3,2,1,0:T(8,128)S(1)}, f32[4,8,26,1]{3,2,1,0:T(8,128)S(1)}, u32[]{:S(2)}, u32[]{:S(2)}) collective-permute-start(f32[4,8,26,1]{3,2,1,0:T(8,128)S(1)} %get-tuple-element.45), channel_id=1, source_target_pairs={{0,1},{1,2},{2,3},{3,4},{4,5},{5,6},{6,7},{8,9},{9,10},{10,11},{11... | collective-permute-start | bytes 9992 | tf_op jit(solution)/shard_map/ppermute | solution.py:19
  270.5 5.2 %collective-permute-done.17 = f32[4,8,26,1]{3,2,1,0:T(8,128)S(1)} collective-permute-done((f32[4,8,26,1]{3,2,1,0:T(8,128)S(1)}, f32[4,8,26,1]{3,2,1,0:T(8,128)S(1)}, u32[]{:S(2)}, u32[]{:S(2)}) %collective-permute-start.17) | collective-permute-done | bytes 3360 | tf_op jit(solution)/shard_map/ppermute | solution.py:20
  275.7 8.2 %collective-permute-done.18 = f32[4,8,26,1]{3,2,1,0:T(8,128)S(1)} collective-permute-done((f32[4,8,26,1]{3,2,1,0:T(8,128)S(1)}, f32[4,8,26,1]{3,2,1,0:T(8,128)S(1)}, u32[]{:S(2)}, u32[]{:S(2)}) %collective-permute-start.18) | collective-permute-done | bytes 3360 | tf_op jit(solution)/shard_map/ppermute | solution.py:19
  (128 shorter events, 46.4 us)
Async XLA Ops:
  7.2 39.8 %all-reduce.2.cloned.1.call-start = ((), (), s32[]{:S(2)}) async-start(), calls=%async_computation | async-start | bytes 196608 | tf_op jit(solution)/shard_map/psum | solution.py:85
  7.9 5.9 %copy-start = (f32[4,8,24,384]{3,2,1,0:T(8,128)S(1)}, f32[4,8,24,384]{3,2,1,0:T(8,128)}, u32[]{:S(2)}) copy-start(f32[4,8,24,384]{3,2,1,0:T(8,128)} %param.5) | copy-start | bytes 3538948
  9.4 5.9 %copy-start.1 = (f32[4,8,24,384]{3,2,1,0:T(8,128)S(1)}, f32[4,8,24,384]{3,2,1,0:T(8,128)}, u32[]{:S(2)}) copy-start(f32[4,8,24,384]{3,2,1,0:T(8,128)} %param.4) | copy-start | bytes 3538948
  10.0 8.1 %collective-permute-start = (f32[2,4,8,24]{2,1,0,3:T(4,128)S(1)}, f32[2,4,8,24]{2,1,0,3:T(4,128)S(1)}, u32[]{:S(2)}, u32[]{:S(2)}) collective-permute-start(f32[2,4,8,24]{2,1,0,3:T(4,128)S(1)} %copy.42), channel_id=1, source_target_pairs={{0,1},{1,0},{2,3},{3,2},{4,5},{5,4},{6,7},{7,6},{8,9},{9,8},{10,11... | collective-permute-start | bytes 18440 | tf_op jit(solution)/shard_map/ppermute | solution.py:94
  15.2 273.1 %all-gather.2.cloned.1.call-start = ((), (), s32[]{:S(2)}) async-start(), calls=%async_computation.1 | async-start | bytes 1474560 | tf_op jit(solution)/shard_map/all_gather | solution.py:129
  15.4 23.4 %collective-permute-start.3 = (f32[4,8,1,384]{3,2,1,0:T(1,128)S(1)}, f32[4,8,1,384]{3,2,1,0:T(1,128)S(1)}, u32[]{:S(2)}, u32[]{:S(2)}) collective-permute-start(f32[4,8,1,384]{3,2,1,0:T(1,128)S(1)} %get-tuple-element.68), channel_id=1, source_target_pairs={{0,8},{8,16},{16,24},{1,9},{9,17},{17,25},{2,10},{10,18},{18,26},{... | collective-permute-start | bytes 147464 | tf_op jit(solution)/shard_map/ppermute | solution.py:19
  16.8 21.9 %collective-permute-start.4 = (f32[4,8,1,384]{3,2,1,0:T(1,128)S(1)}, f32[4,8,1,384]{3,2,1,0:T(1,128)S(1)}, u32[]{:S(2)}, u32[]{:S(2)}) collective-permute-start(f32[4,8,1,384]{3,2,1,0:T(1,128)S(1)} %get-tuple-element.69), channel_id=1, source_target_pairs={{8,0},{16,8},{24,16},{9,1},{17,9},{25,17},{10,2},{18,10},{26,18},{... | collective-permute-start | bytes 147464 | tf_op jit(solution)/shard_map/ppermute | solution.py:20
  18.2 4.7 %collective-permute-start.1 = (f32[2,4,8,24]{2,1,0,3:T(4,128)S(1)}, f32[2,4,8,24]{2,1,0,3:T(4,128)S(1)}, u32[]{:S(2)}, u32[]{:S(2)}) collective-permute-start(f32[2,4,8,24]{2,1,0,3:T(4,128)S(1)} %add.119), channel_id=1, source_target_pairs={{0,2},{1,3},{2,0},{3,1},{4,6},{5,7},{6,4},{7,5},{8,10},{9,11},{10,... | collective-permute-start | bytes 18440 | tf_op jit(solution)/shard_map/ppermute | solution.py:94
  22.9 8.3 %collective-permute-start.2 = (f32[2,4,8,24]{2,1,0,3:T(4,128)S(1)}, f32[2,4,8,24]{2,1,0,3:T(4,128)S(1)}, u32[]{:S(2)}, u32[]{:S(2)}) collective-permute-start(f32[2,4,8,24]{2,1,0,3:T(4,128)S(1)} %add.120), channel_id=1, source_target_pairs={{0,4},{1,5},{2,6},{3,7},{4,0},{5,1},{6,2},{7,3},{8,12},{9,13},{10,... | collective-permute-start | bytes 18440 | tf_op jit(solution)/shard_map/ppermute | solution.py:94
  40.0 60.0 %collective-permute-start.5 = (f32[4,8,26,1]{3,2,1,0:T(8,128)}, f32[4,8,26,1]{3,2,1,0:T(8,128)}, u32[]{:S(2)}, u32[]{:S(2)}) collective-permute-start(f32[4,8,26,1]{3,2,1,0:T(8,128)} %get-tuple-element.50), channel_id=1, source_target_pairs={{0,1},{1,2},{2,3},{3,4},{4,5},{5,6},{6,7},{8,9},{9,10},{10,11},{11... | collective-permute-start | bytes 9992 | tf_op jit(solution)/shard_map/ppermute | solution.py:19
  43.2 56.7 %collective-permute-start.6 = (f32[4,8,26,1]{3,2,1,0:T(8,128)}, f32[4,8,26,1]{3,2,1,0:T(8,128)}, u32[]{:S(2)}, u32[]{:S(2)}) collective-permute-start(f32[4,8,26,1]{3,2,1,0:T(8,128)} %get-tuple-element.51), channel_id=1, source_target_pairs={{1,0},{2,1},{3,2},{4,3},{5,4},{6,5},{7,6},{9,8},{10,9},{11,10},{12... | collective-permute-start | bytes 9992 | tf_op jit(solution)/shard_map/ppermute | solution.py:20
  105.4 9.0 %collective-permute-start.7 = (f32[4,8,1,384]{3,2,1,0:T(1,128)S(1)}, f32[4,8,1,384]{3,2,1,0:T(1,128)S(1)}, u32[]{:S(2)}, u32[]{:S(2)}) collective-permute-start(f32[4,8,1,384]{3,2,1,0:T(1,128)S(1)} %get-tuple-element.64), channel_id=1, source_target_pairs={{0,8},{8,16},{16,24},{1,9},{9,17},{17,25},{2,10},{10,18},{18,26},{... | collective-permute-start | bytes 147464 | tf_op jit(solution)/shard_map/ppermute | solution.py:19
  106.7 7.7 %collective-permute-start.8 = (f32[4,8,1,384]{3,2,1,0:T(1,128)S(1)}, f32[4,8,1,384]{3,2,1,0:T(1,128)S(1)}, u32[]{:S(2)}, u32[]{:S(2)}) collective-permute-start(f32[4,8,1,384]{3,2,1,0:T(1,128)S(1)} %get-tuple-element.65), channel_id=1, source_target_pairs={{8,0},{16,8},{24,16},{9,1},{17,9},{25,17},{10,2},{18,10},{26,18},{... | collective-permute-start | bytes 147464 | tf_op jit(solution)/shard_map/ppermute | solution.py:20
  108.0 156.3 %collective-permute-start.15 = (f32[4,8,1,384]{3,2,1,0:T(1,128)}, f32[4,8,1,384]{3,2,1,0:T(1,128)S(1)}, u32[]{:S(2)}, u32[]{:S(2)}) collective-permute-start(f32[4,8,1,384]{3,2,1,0:T(1,128)} %get-tuple-element.59), channel_id=1, source_target_pairs={{8,0},{16,8},{24,16},{9,1},{17,9},{25,17},{10,2},{18,10},{26,18},{... | collective-permute-start | bytes 147464 | tf_op jit(solution)/shard_map/ppermute | solution.py:20
  109.3 155.0 %collective-permute-start.16 = (f32[4,8,1,384]{3,2,1,0:T(1,128)}, f32[4,8,1,384]{3,2,1,0:T(1,128)S(1)}, u32[]{:S(2)}, u32[]{:S(2)}) collective-permute-start(f32[4,8,1,384]{3,2,1,0:T(1,128)} %get-tuple-element.58), channel_id=1, source_target_pairs={{0,8},{8,16},{16,24},{1,9},{9,17},{17,25},{2,10},{10,18},{18,26},{... | collective-permute-start | bytes 147464 | tf_op jit(solution)/shard_map/ppermute | solution.py:19
  114.7 16.0 %collective-permute-start.10 = (f32[4,8,26,1]{3,2,1,0:T(8,128)S(1)}, f32[4,8,26,1]{3,2,1,0:T(8,128)S(1)}, u32[]{:S(2)}, u32[]{:S(2)}) collective-permute-start(f32[4,8,26,1]{3,2,1,0:T(8,128)S(1)} %get-tuple-element.49), channel_id=1, source_target_pairs={{1,0},{2,1},{3,2},{4,3},{5,4},{6,5},{7,6},{9,8},{10,9},{11,10},{12... | collective-permute-start | bytes 9992 | tf_op jit(solution)/shard_map/ppermute | solution.py:20
  116.0 22.3 %collective-permute-start.9 = (f32[4,8,26,1]{3,2,1,0:T(8,128)S(1)}, f32[4,8,26,1]{3,2,1,0:T(8,128)S(1)}, u32[]{:S(2)}, u32[]{:S(2)}) collective-permute-start(f32[4,8,26,1]{3,2,1,0:T(8,128)S(1)} %get-tuple-element.48), channel_id=1, source_target_pairs={{0,1},{1,2},{2,3},{3,4},{4,5},{5,6},{6,7},{8,9},{9,10},{10,11},{11... | collective-permute-start | bytes 9992 | tf_op jit(solution)/shard_map/ppermute | solution.py:19
  143.2 4.0 %collective-permute-start.11 = (f32[4,8,1,384]{3,2,1,0:T(1,128)S(1)}, f32[4,8,1,384]{3,2,1,0:T(1,128)S(1)}, u32[]{:S(2)}, u32[]{:S(2)}) collective-permute-start(f32[4,8,1,384]{3,2,1,0:T(1,128)S(1)} %get-tuple-element.62), channel_id=1, source_target_pairs={{0,8},{8,16},{16,24},{1,9},{9,17},{17,25},{2,10},{10,18},{18,26},{... | collective-permute-start | bytes 147464 | tf_op jit(solution)/shard_map/ppermute | solution.py:19
  145.3 3.4 %collective-permute-start.12 = (f32[4,8,1,384]{3,2,1,0:T(1,128)S(1)}, f32[4,8,1,384]{3,2,1,0:T(1,128)S(1)}, u32[]{:S(2)}, u32[]{:S(2)}) collective-permute-start(f32[4,8,1,384]{3,2,1,0:T(1,128)S(1)} %get-tuple-element.63), channel_id=1, source_target_pairs={{8,0},{16,8},{24,16},{9,1},{17,9},{25,17},{10,2},{18,10},{26,18},{... | collective-permute-start | bytes 147464 | tf_op jit(solution)/shard_map/ppermute | solution.py:20
  149.0 26.0 %collective-permute-start.13 = (f32[4,8,26,1]{3,2,1,0:T(8,128)S(1)}, f32[4,8,26,1]{3,2,1,0:T(8,128)S(1)}, u32[]{:S(2)}, u32[]{:S(2)}) collective-permute-start(f32[4,8,26,1]{3,2,1,0:T(8,128)S(1)} %get-tuple-element.46), channel_id=1, source_target_pairs={{0,1},{1,2},{2,3},{3,4},{4,5},{5,6},{6,7},{8,9},{9,10},{10,11},{11... | collective-permute-start | bytes 9992 | tf_op jit(solution)/shard_map/ppermute | solution.py:19
  153.5 21.6 %collective-permute-start.14 = (f32[4,8,26,1]{3,2,1,0:T(8,128)S(1)}, f32[4,8,26,1]{3,2,1,0:T(8,128)S(1)}, u32[]{:S(2)}, u32[]{:S(2)}) collective-permute-start(f32[4,8,26,1]{3,2,1,0:T(8,128)S(1)} %get-tuple-element.47), channel_id=1, source_target_pairs={{1,0},{2,1},{3,2},{4,3},{5,4},{6,5},{7,6},{9,8},{10,9},{11,10},{12... | collective-permute-start | bytes 9992 | tf_op jit(solution)/shard_map/ppermute | solution.py:20
  180.6 8.4 %copy-start.2 = (f32[1,8,24,384]{3,2,1,0:T(8,128)}, f32[1,8,24,384]{3,2,1,0:T(8,128)S(1)}, u32[]{:S(2)}) copy-start(f32[1,8,24,384]{3,2,1,0:T(8,128)S(1)} %get-tuple-element.11) | copy-start | bytes 884740
  264.6 11.1 %collective-permute-start.17 = (f32[4,8,26,1]{3,2,1,0:T(8,128)S(1)}, f32[4,8,26,1]{3,2,1,0:T(8,128)S(1)}, u32[]{:S(2)}, u32[]{:S(2)}) collective-permute-start(f32[4,8,26,1]{3,2,1,0:T(8,128)S(1)} %get-tuple-element.44), channel_id=1, source_target_pairs={{1,0},{2,1},{3,2},{4,3},{5,4},{6,5},{7,6},{9,8},{10,9},{11,10},{12... | collective-permute-start | bytes 9992 | tf_op jit(solution)/shard_map/ppermute | solution.py:20
  265.9 18.0 %collective-permute-start.18 = (f32[4,8,26,1]{3,2,1,0:T(8,128)S(1)}, f32[4,8,26,1]{3,2,1,0:T(8,128)S(1)}, u32[]{:S(2)}, u32[]{:S(2)}) collective-permute-start(f32[4,8,26,1]{3,2,1,0:T(8,128)S(1)} %get-tuple-element.45), channel_id=1, source_target_pairs={{0,1},{1,2},{2,3},{3,4},{4,5},{5,6},{6,7},{8,9},{9,10},{10,11},{11... | collective-permute-start | bytes 9992 | tf_op jit(solution)/shard_map/ppermute | solution.py:19
  (7 other events, 7.3 us)
Sparse Core Ops, SparseCore 0:
  15.3 31.5 all-reduce.1
  264.3 15.4 all-gather.1
